TPU v7x, 32 devices: a whole 2x2x4 slice. The times are simulated.
32 devices in a mesh: fsdp: 16 (over z, y, x), tp: 2 (over core).
Axes of the slice: x: 2, y: 2, z: 4, core: 2. Of those that a mesh axis runs over, the one named last changes fastest.
Arguments:
- gradient: bfloat16 [2, 8192, 8192], P(None, 'fsdp', 'tp'), may hold values from -2764800 to 2764800
- momentum: float32 [2, 8192, 8192], P(None, 'fsdp', 'tp'), may hold values from -36 to 36
- right_basis_old: float32 [2, 512, 8192], P(None, 'fsdp', 'tp'), may hold values from -6 to 6
- token_counts: int32 [32], P(('fsdp', 'tp')), may hold values from 400 to 6397, as said below
Outputs:
- momentum_corrected: float32 [2, 8192, 8192], P(None, 'fsdp', 'tp')
- direction: float32 [2, 8192, 8192], P(None, 'fsdp', 'tp')
- right_basis_new: float32 [2, 512, 8192], P(None, 'fsdp', 'tp')
Inputs may be any that keep to these rules, and one draw needn't show every extreme that they name: `token_counts`: each device's count; the first entry is 400.
All inputs are finite; a program needn't handle non-finite values.
Results may differ from a plain program's by a relative error of at most 0.0003.
Values sent between devices are 32-bit elements; how exact they have to be, the bound alone decides.
A program may use at most 256 MiB of HBM per device.

v0:
```python
import math

import jax
import jax.numpy as jnp
from jax import lax
from jax.sharding import PartitionSpec as P

MODEL_WIDTH = 8192
UPDATE_RANK = 512


epsilon = 1e-06
retained_fraction = 0.05
top_precision = lax.Precision.HIGHEST


def orthonormalize(factor, momentum_product):
    return jax.scipy.linalg.solve_triangular(factor, momentum_product.T, lower=True).T


def per_device(gradient, momentum, right_basis_old, token_counts):
    token_total = lax.psum(jnp.sum(token_counts.astype(jnp.float32)), ("fsdp", "tp"))
    momentum_store = momentum + gradient.astype(jnp.float32) / token_total
    partial_rows = jnp.einsum(
        "mij,mkj->mik",
        momentum_store,
        lax.all_gather(right_basis_old, "fsdp", axis=1, tiled=True),
        precision=top_precision,
    )
    momentum_product = lax.psum(partial_rows, "tp")
    shard_products = jnp.einsum(
        "eut,eug->etg", momentum_product, momentum_product, precision=top_precision
    )
    inner_products = lax.psum(shard_products, "fsdp")
    factor = jnp.linalg.cholesky(inner_products)
    orthogonal_factor = jax.vmap(orthonormalize)(factor, momentum_product)
    reduced_local = lax.psum_scatter(
        jnp.einsum("ksf,ksu->fku", orthogonal_factor, momentum_store, precision=top_precision),
        "fsdp",
        scatter_dimension=0,
        tiled=True,
    )
    squares = lax.psum(jnp.sum(reduced_local * reduced_local, axis=2), "tp")
    local_rms = jnp.sqrt(squares / MODEL_WIDTH + epsilon)
    unit_local = reduced_local / local_rms[:, :, None]
    normalized_whole, row_rms = (
        lax.all_gather(unit_local, "fsdp", axis=0, tiled=True),
        lax.all_gather(local_rms, "fsdp", axis=0, tiled=True),
    )
    product_total = normalized_whole * row_rms[:, :, None]
    momentum_corrected = momentum_store - retained_fraction * jnp.einsum(
        "lnp,plu->lnu", orthogonal_factor, product_total, precision=top_precision
    )
    direction = math.sqrt(MODEL_WIDTH / UPDATE_RANK) * jnp.einsum(
        "lnp,plu->lnu", orthogonal_factor, normalized_whole, precision=top_precision
    )
    right_basis_new = jnp.transpose(unit_local, (1, 0, 2))
    return (momentum_corrected, direction, right_basis_new)


def solution(mesh):
    in_specs = (
        P(None, "fsdp", "tp"),
        P(None, "fsdp", "tp"),
        P(None, "fsdp", "tp"),
        P(("fsdp", "tp")),
    )
    out_specs = (P(None, "fsdp", "tp"), P(None, "fsdp", "tp"), P(None, "fsdp", "tp"))
    return jax.shard_map(
        per_device, mesh=mesh, in_specs=in_specs, out_specs=out_specs, check_vma=False
    )
```

profile of v0, /device:TPU:0, one launch (start us, length us, event | category | flops | bytes accessed | tf_op | source)
XLA Modules:
  0.0 1508.6 jit_solution(1823425082048597385)
XLA Ops:
  7.2 0.7 all-gather.4.cloned.1.call-update
  8.6 44.4 %psum.28 = f32[]{:T(128)} all-reduce(f32[]{:T(128)} %bitcast), channel_id=1, replica_groups=mesh['fsdp'=16,'tp'=2] {'fsdp','tp'}, use_global_device_ids=true, to_apply=%region_0.0 | all-reduce | flops 1 | bytes 8 | tf_op jit(solution)/shard_map/psum | solution.py:22
  53.0 153.3 %all-gather.4.cloned.1.call-done = f32[2,512,4096]{2,1,0:T(8,128)} async-done(((f32[2,32,4096]{2,1,0:T(8,128)}), f32[2,512,4096]{2,1,0:T(8,128)}) %all-gather.4.cloned.1.call-update) | async-done | bytes 16777232 | tf_op jit(solution)/shard_map/all_gather | solution.py:27
  206.3 34.0 %fusion.47 = f32[2,512,512]{2,1,0:T(8,128)} fusion(f32[2,512,4096]{2,1,0:T(8,128)} %all-gather.4.cloned.1.call-done, f32[2,512,4096]{2,1,0:T(8,128)} %param.5, bf16[2,512,4096]{2,1,0:T(8,128)(2,1)} %param.4, f32[]{:T(128)} %psum.28), kind=kOutput, calls=%fused_computation.84 | convolution fusion | flops 25782386688 | bytes 44040196 | tf_op jit(solution)/shard_map/mij,mkj->mik/dot_general | solution.py:24
  240.4 19.5 %all-reduce.6.cloned.1.call-done = f32[2,512,512]{2,1,0:T(8,128)} async-done(((f32[2,512,512]{2,1,0:T(8,128)}), f32[2,512,512]{2,1,0:T(8,128)}) %all-reduce.6.cloned.1.call-update) | async-done | bytes 2097168 | tf_op jit(solution)/shard_map/psum | solution.py:30
  259.9 7.1 fusion.49
  267.0 0.2 all-reduce.10.cloned.1.call-start
  267.3 126.9 %all-reduce.8.cloned.1.call-done = f32[2,512,512]{1,2,0:T(8,128)} async-done(((f32[2,512,512]{1,2,0:T(8,128)}), f32[2,512,512]{1,2,0:T(8,128)}) %all-reduce.8.cloned.1.call-update) | async-done | bytes 2097168 | tf_op jit(solution)/shard_map/psum | solution.py:34
  394.3 3.0 copy.151
  397.3 2.1 fusion.9
  399.4 1.3 copy-done.3
  400.7 23.5 %custom-call.35 = f32[2,128,128]{2,1,0:T(8,128)S(1)} custom-call(f32[2,128,128]{2,1,0:T(8,128)S(1)} %cholesky.274), custom_call_target="Cholesky" | custom-call | tf_op jit(solution)/shard_map/jit(cholesky)/cholesky | solution.py:35
  424.2 19.7 %custom-call.36 = f32[2,1,128,128]{2,3,1,0:T(8,128)S(1)} custom-call(f32[2,1,128,128]{3,2,1,0:T(8,128)S(1)} %select_bitcast_fusion.2), custom_call_target="InvertDiagBlocksLowerTriangular" | custom-call | tf_op jit(solution)/shard_map/jit(cholesky)/cholesky | solution.py:35
  443.9 0.3 cholesky.234
  444.2 1.5 constant_dynamic-update-slice_fusion.3
  445.7 1.5 convolution_subtract_fusion.2
  447.2 23.5 %custom-call.37 = f32[2,128,128]{2,1,0:T(8,128)S(1)} custom-call(f32[2,128,128]{2,1,0:T(8,128)S(1)} %cholesky.278), custom_call_target="Cholesky" | custom-call | tf_op jit(solution)/shard_map/jit(cholesky)/cholesky | solution.py:35
  470.7 20.1 %custom-call.38 = f32[2,1,128,128]{2,3,1,0:T(8,128)S(1)} custom-call(f32[2,1,128,128]{3,2,1,0:T(8,128)S(1)} %get-tuple-element.46), custom_call_target="InvertDiagBlocksLowerTriangular" | custom-call | tf_op jit(solution)/shard_map/jit(cholesky)/cholesky | solution.py:35
  490.8 0.4 convolution_dynamic-update-slice_fusion
  491.2 1.6 convolution_subtract_fusion.3
  492.7 23.5 %custom-call.39 = f32[2,128,128]{2,1,0:T(8,128)S(1)} custom-call(f32[2,128,128]{2,1,0:T(8,128)S(1)} %cholesky.283), custom_call_target="Cholesky" | custom-call | tf_op jit(solution)/shard_map/jit(cholesky)/cholesky | solution.py:35
  516.2 19.7 %custom-call.40 = f32[2,1,128,128]{2,3,1,0:T(8,128)S(1)} custom-call(f32[2,1,128,128]{3,2,1,0:T(8,128)S(1)} %get-tuple-element.44), custom_call_target="InvertDiagBlocksLowerTriangular" | custom-call | tf_op jit(solution)/shard_map/jit(cholesky)/cholesky | solution.py:35
  535.9 0.3 convolution_dynamic-update-slice_fusion.1
  536.2 1.5 convolution_subtract_fusion.4
  537.7 23.6 %custom-call.41 = f32[2,128,128]{2,1,0:T(8,128)S(1)} custom-call(f32[2,128,128]{2,1,0:T(8,128)S(1)} %convolution_subtract_fusion.4), custom_call_target="Cholesky" | custom-call | tf_op jit(solution)/shard_map/jit(cholesky)/cholesky | solution.py:35
  561.4 0.1 compare_reduce_fusion.2
  561.6 0.2 compare_reduce_fusion
  561.8 1.0 copy-done.1
  562.7 3.5 select_select_fusion
  566.2 14.2 while.1
  566.3 0.5 fusion.60
  566.8 3.0 bitcast_dynamic-update-slice_fusion.2
  569.9 0.5 fusion.60
  570.4 3.0 bitcast_dynamic-update-slice_fusion.2
  573.4 0.5 fusion.60
  574.0 3.0 bitcast_dynamic-update-slice_fusion.2
  577.0 0.5 fusion.60
  577.6 2.9 bitcast_dynamic-update-slice_fusion.2
  580.5 79.4 %custom-call.42 = f32[2,4,128,128]{2,3,1,0:T(8,128)S(1)} custom-call(f32[2,4,128,128]{3,2,1,0:T(8,128)} %bitcast.75), custom_call_target="InvertDiagBlocksLowerTriangular" | custom-call | tf_op jit(solution)/shard_map/vmap(jit(_solve_triangular))/triangular_solve | solution.py:18
  659.9 0.7 fusion.22
  660.6 0.1 copy-done.6
  660.7 1.9 convolution_subtract_fusion.1
  662.6 1.6 fusion.35
  664.2 2.8 convolution_subtract_fusion
  667.1 0.6 fusion.33
  667.7 3.9 fusion.16
  671.6 0.6 fusion.32
  672.3 59.0 %convolution_bitcast_fusion = f32[512,2,4096]{0,2,1:T(8,128)} fusion(f32[2,128,512]{2,1,0:T(8,128)S(1)} %fusion.32, f32[2,128,512]{2,1,0:T(8,128)S(1)} %fusion.33, f32[2,128,512]{2,1,0:T(8,128)S(1)} %fusion.35, f32[2,128,512]{2,1,0:T(8,128)S(1)} %fusion.22, f32[2,512,4096]{2,1,0:T(8,128)} %param.5, bf16[2,512,4096]{2,1,0:T(8,128)(2,1)} %param.4, f32[]{:T(128)} %psum.28), kind=kOutput, calls=%fused_computation.8 | convolution fusion | flops 25783959552 | bytes 44040196 | tf_op jit(solution)/shard_map/ksf,ksu->fku/dot_general | solution.py:38
  731.3 25.3 %copy.171 = f32[512,2,4096]{2,1,0:T(2,128)} copy(f32[512,2,4096]{0,2,1:T(8,128)} %convolution_bitcast_fusion) | data formatting | bytes 33554432 | tf_op jit(solution)/shard_map/ksf,ksu->fku/transpose | solution.py:38
  756.7 0.6 copy-done.8
  757.2 0.6 dynamic-slice.4
  758.5 453.3 %all-reduce.10.cloned.1.call-done = f32[512,2,4096]{2,1,0:T(2,128)} async-done(((f32[512,2,4096]{2,1,0:T(2,128)}), f32[512,2,4096]{2,1,0:T(2,128)}) %all-reduce.10.cloned.1.call-update) | async-done | bytes 16777232
  1211.7 1.7 multiply_reduce_fusion
  1213.5 2.4 psum.31
  1216.0 0.1 copy.173
  1216.1 2.8 dynamic-slice_divide_fusion
  1218.9 39.2 %all-gather = f32[16,32,2]{1,2,0:T(2,128)S(1)} all-gather(f32[1,32,2]{1,2,0:T(2,128)S(1)} %get-tuple-element.48), channel_id=1, replica_groups=mesh['fsdp'=16,'tp'=2] {'fsdp'}, dimensions={0}, use_global_device_ids=true | all-gather | bytes 4352 | tf_op jit(solution)/shard_map/all_gather | solution.py:48
  1258.1 0.2 copy.200
  1258.3 2.1 fusion.58
  1260.4 1.6 copy.180
  1262.0 147.8 %all-gather.6.cloned.1.call-done = f32[512,2,4096]{2,1,0:T(2,128)} async-done(((f32[32,2,4096]{2,1,0:T(2,128)}), f32[512,2,4096]{2,1,0:T(2,128)}) %all-gather.6.cloned.1.call-update) | async-done | bytes 16777232 | tf_op jit(solution)/shard_map/all_gather | solution.py:47
  1409.8 12.3 broadcast_multiply_fusion
  1422.1 41.7 %multiply_subtract_fusion = f32[2,512,4096]{2,1,0:T(8,128)} fusion(f32[512,2,4096]{2,1,0:T(2,128)} %broadcast_multiply_fusion, f32[2,128,512]{2,1,0:T(8,128)S(1)} %fusion.32, f32[2,128,512]{2,1,0:T(8,128)S(1)} %copy-done.5, f32[2,128,512]{2,1,0:T(8,128)S(1)} %fusion.35, f32[2,128,512]{2,1,0:T(8,128)S(1)} %fusion.22, f32[2,512,4096]{2,1,0:T(8,128)} %param.5, ...), kind=kOutput, calls=%fused_computation.6 | convolution fusion | flops 25792348160 | bytes 60817412 | tf_op jit(solution)/shard_map/lnp,plu->lnu/dot_general | solution.py:51
  1463.8 38.1 %fusion.6 = f32[2,512,4096]{2,1,0:T(8,128)} fusion(f32[512,2,4096]{2,1,0:T(2,128)} %all-gather.6.cloned.1.call-done, f32[2,128,512]{2,1,0:T(8,128)S(1)} %fusion.32, f32[2,128,512]{2,1,0:T(8,128)S(1)} %copy-done.5, f32[2,128,512]{2,1,0:T(8,128)S(1)} %fusion.35, f32[2,128,512]{2,1,0:T(8,128)S(1)} %fusion.22), kind=kOutput, calls=%fused_computation.9 | convolution fusion | flops 25775570944 | bytes 35651584 | tf_op jit(solution)/shard_map/lnp,plu->lnu/dot_general | solution.py:54
  (42 shorter events, 0.9 us)
Async XLA Ops:
  7.2 199.1 %all-gather.4.cloned.1.call-start = ((), (), s32[]{:S(2)}) async-start(), calls=%async_computation | async-start | bytes 17825792 | tf_op jit(solution)/shard_map/all_gather | solution.py:27
  7.9 252.0 %all-reduce.6.cloned.1.call-start = ((), (), s32[]{:S(2)}) async-start(), calls=%async_computation.1 | async-start | bytes 4194304 | tf_op jit(solution)/shard_map/psum | solution.py:30
  240.3 154.0 %all-reduce.8.cloned.1.call-start = ((), (), s32[]{:S(2)}) async-start(), calls=%async_computation.2 | async-start | bytes 4194304 | tf_op jit(solution)/shard_map/psum | solution.py:34
  267.0 944.8 %all-reduce.10.cloned.1.call-start = ((), (), s32[]{:S(2)}) async-start(), calls=%async_computation.4 | async-start | bytes 33554432
  394.3 3.0 copy-start.2
  399.4 1.3 copy-start.3
  561.4 1.3 copy-start.1
  562.7 97.2 %copy-start = (f32[2,512,512]{2,1,0:T(8,128)S(1)}, f32[2,512,512]{2,1,0:T(8,128)}, u32[]{:S(2)}) copy-start(f32[2,512,512]{2,1,0:T(8,128)} %all-reduce.6.cloned.1.call-done) | copy-start | bytes 6291460
  659.9 0.8 copy-start.6
  662.6 4.5 copy-start.7
  667.7 4.6 copy-start.4
  756.6 0.7 copy-start.8
  756.6 653.2 %all-gather.6.cloned.1.call-start = ((), (), s32[]{:S(2)}) async-start(), calls=%async_computation.3 | async-start | bytes 17825792 | tf_op jit(solution)/shard_map/all_gather | solution.py:47
  1409.8 12.3 copy-start.5
Sparse Core Ops, SparseCore 0:
  10.8 195.4 all-gather.3
  240.4 19.3 all-reduce.5
  267.1 127.1 all-reduce.7
  756.7 454.9 all-reduce.9
  1219.1 190.6 all-gather.5
where the time goes:
time: 1520 us; the launch traced here: 1510 us
  waiting for transfers between devices  902 us (59%)
  other arithmetic  258 us (17%)
  matrix products  199 us (13%)
  blocking collectives  86 us (6%)
  local copies, waits for them, and re-layouts  48.4 us (3%)
  between operations  15.6 us (1%)
    unnamed x6, waiting for transfers between devices  454 us
    another operation x16, other arithmetic, per_device(): factor = jnp.linalg.cholesky(inner_products)  154 us
    all_gather x1, waiting for transfers between devices, per_device(): lax.all_gather(right_basis_old, 'fsdp', axis=1, tiled=True)  153 us
    all_gather x1, waiting for transfers between devices, per_device(): lax.all_gather(unit_local, 'fsdp', axis=0, tiled=True)  148 us
    psum x1, waiting for transfers between devices, per_device(): inner_products = lax.psum(shard_products, 'fsdp')  127 us
    another operation x4, other arithmetic, orthonormalize(): jax.scipy.linalg.solve_triangular(factor, momentum_product.T, lower=True)  83 us
    dot_general x1, matrix products, per_device(): jnp.einsum('ksf,ksu->fku', orthogonal_factor, momentum_store, precision=t...  59 us
    psum x1, blocking collectives, per_device(): lax.psum(jnp.sum(token_counts.astype(jnp.float32)), ('fsdp', 'tp'))  44.4 us
  transfers between devices with their start and end apart: 5, of which 5 were waited for; matrix products, arithmetic and copies ran while one was open for 0% of the time, Pallas kernels for 0%

commit v1 on v0

v1 whole, which is shorter than its diff:
```python
import functools
import math

import jax
import jax.numpy as jnp
from jax import lax
from jax.experimental import pallas as pl
from jax.experimental.pallas import tpu as pltpu
from jax.sharding import PartitionSpec as P

epsilon = 1e-06
retained_fraction = 0.05
top_precision = lax.Precision.HIGHEST
good_precision = lax.Precision.HIGH
MESH = pl.DeviceIdType.MESH
PANEL = 128


def place_of(device, n):
    if n != 16:
        return device
    z, y, x = device // 4, (device // 2) % 2, device % 2
    column = 3 * y + x - 2 * x * y
    along = z + (column % 2) * (3 - 2 * z)
    return column * 4 + along


def device_at(place, n):
    if n != 16:
        return place
    column, along = place // 4, place % 4
    z = along + (column % 2) * (3 - 2 * along)
    x, y = ((column + 1) // 2) % 2, column // 2
    return z * 4 + y * 2 + x


def scatter_kernel(n, halves, terms, out, slots, send_sem, recv_sem):
    me = lax.axis_index("fsdp")
    place = place_of(me, n)
    right = device_at((place + 1) % n, n)
    left = device_at((place + n - 1) % n, n)
    rows, width = out.shape[1], out.shape[2] // halves

    barrier = pltpu.get_barrier_semaphore()
    for neighbour in (left, right):
        pl.semaphore_signal(barrier, inc=1, device_id={"fsdp": neighbour}, device_id_type=MESH)
    pl.semaphore_wait(barrier, 2)

    streams = [(mat, half) for half in range(halves) for mat in range(2)]

    def rows_at(mat, step):
        if mat == 0:
            block = device_at((place + 2 * n - 1 - step) % n, n)
        else:
            block = device_at((place + 1 + step) % n, n)
        return pl.ds(pl.multiple_of(block * rows, rows), rows)

    def copy(mat, half, step, source):
        columns = pl.ds(half * width, width)
        stream = mat * halves + half
        return pltpu.make_async_remote_copy(
            src_ref=source,
            dst_ref=slots.at[step, mat, :, columns],
            send_sem=send_sem.at[stream, step],
            recv_sem=recv_sem.at[stream, step],
            device_id={"fsdp": right if mat == 0 else left},
            device_id_type=MESH,
        )

    def held(mat, half, step):
        return slots.at[step, mat, :, pl.ds(half * width, width)]

    for mat, half in streams:
        copy(mat, half, 0, terms.at[mat, rows_at(mat, 0), pl.ds(half * width, width)]).start()

    def step_body(step, carry):
        for mat, half in streams:
            columns = pl.ds(half * width, width)
            before = held(mat, half, step - 1)
            copy(mat, half, step - 1, before).wait_recv()
            slots[step - 1, mat, :, columns] = (
                slots[step - 1, mat, :, columns] + terms[mat, rows_at(mat, step), columns]
            )
            copy(mat, half, step, before).start()
        return carry

    lax.fori_loop(1, n - 1, step_body, 0)
    for mat, half in streams:
        columns = pl.ds(half * width, width)
        copy(mat, half, n - 2, held(mat, half, n - 2)).wait_recv()
        out[mat, :, columns] = slots[n - 2, mat, :, columns] + terms[mat, rows_at(mat, n - 1), columns]

    def drain(step, carry):
        for mat, half in streams:
            copy(mat, half, step, held(mat, half, step)).wait_send()
        return carry

    lax.fori_loop(0, n - 1, drain, 0)


def ring_scatter(terms, n):
    mats, rank, width = terms.shape
    rows, halves = rank // n, 2
    return pl.pallas_call(
        functools.partial(scatter_kernel, n, halves),
        out_shape=jax.ShapeDtypeStruct((mats, rows, width), jnp.float32),
        in_specs=[pl.BlockSpec(memory_space=pltpu.VMEM)],
        out_specs=pl.BlockSpec(memory_space=pltpu.VMEM),
        scratch_shapes=[
            pltpu.VMEM((n - 1, mats, rows, width), jnp.float32),
            pltpu.SemaphoreType.DMA((2 * halves, n - 1)),
            pltpu.SemaphoreType.DMA((2 * halves, n - 1)),
        ],
        cost_estimate=pl.CostEstimate(
            flops=terms.size, bytes_accessed=terms.size * 40, transcendentals=0
        ),
        compiler_params=pltpu.CompilerParams(
            collective_id=0, has_side_effects=True, vmem_limit_bytes=48 * 1024 * 1024
        ),
        name="ring_scatter",
    )(terms)


def dot_top(a, b, contract):
    return lax.dot_general(
        a, b, (contract, ((), ())), precision=top_precision, preferred_element_type=jnp.float32
    )


def factor_panels(panels):
    tiles = PANEL // 8
    row_ids = lax.broadcasted_iota(jnp.int32, (8, PANEL), 0)
    lane_ids = lax.broadcasted_iota(jnp.int32, (8, PANEL), 1)
    state = []
    for panel in panels:
        a = [panel[8 * i : 8 * i + 8, :] for i in range(tiles)]
        x = [jnp.where(lane_ids == row_ids + 8 * i, 1.0, 0.0).astype(jnp.float32) for i in range(tiles)]
        state.append((a, x))
    for j in range(PANEL):
        b, r = j // 8, j % 8
        for a, x in state:
            pivot = jnp.broadcast_to(a[b][r : r + 1, j : j + 1], (1, PANEL))
            scale = lax.rsqrt(pivot)
            scale = scale * (1.5 - 0.5 * pivot * scale * scale)
            row_a = a[b][r : r + 1, :] * scale
            row_x = x[b][r : r + 1, :] * scale
            scaled_a, scaled_x = row_a * scale, row_x * scale
            for i in range(b, tiles):
                if i == b and r == 7:
                    continue
                column = jnp.broadcast_to(a[i][:, j : j + 1], (8, PANEL))
                if i == b:
                    column = jnp.where(row_ids > r, column, 0.0)
                a[i] = a[i] - column * scaled_a
                x[i] = x[i] - column * scaled_x
            a[b] = jnp.where(row_ids == r, row_a, a[b])
            x[b] = jnp.where(row_ids == r, row_x, x[b])
    return [jnp.concatenate(x, axis=0) for _, x in state]


def factor_kernel(gram, inverse, work):
    mats, rank = gram.shape[0], gram.shape[1]
    row_ids = lax.broadcasted_iota(jnp.int32, (rank, rank), 0)
    lane_ids = lax.broadcasted_iota(jnp.int32, (rank, rank), 1)
    for m in range(mats):
        work[m] = gram[m]
        inverse[m] = jnp.where(row_ids == lane_ids, 1.0, 0.0).astype(jnp.float32)

    def diagonal(k, carry):
        at = pl.multiple_of(k * PANEL, PANEL)
        here = pl.ds(at, PANEL)
        lower = factor_panels([work[m, here, here] for m in range(mats)])
        for m in range(mats):
            solved = dot_top(lower[m], work[m, here, :], ((1,), (0,)))
            solved_inverse = dot_top(lower[m], inverse[m, here, :], ((1,), (0,)))
            lanes = lax.broadcasted_iota(jnp.int32, solved.shape, 1)
            below = jnp.where(lanes >= at + PANEL, solved, 0.0)
            work[m] = work[m] - dot_top(below, below, ((0,), (0,)))
            inverse[m] = inverse[m] - dot_top(below, solved_inverse, ((0,), (0,)))
            inverse[m, here, :] = solved_inverse
        return carry

    lax.fori_loop(0, rank // PANEL, diagonal, 0)


def inverse_factor(gram):
    return pl.pallas_call(
        factor_kernel,
        out_shape=jax.ShapeDtypeStruct(gram.shape, jnp.float32),
        in_specs=[pl.BlockSpec(memory_space=pltpu.VMEM)],
        out_specs=pl.BlockSpec(memory_space=pltpu.VMEM),
        scratch_shapes=[pltpu.VMEM(gram.shape, jnp.float32)],
        cost_estimate=pl.CostEstimate(flops=80_000_000_000, bytes_accessed=4 << 20, transcendentals=0),
        compiler_params=pltpu.CompilerParams(vmem_limit_bytes=40 * 1024 * 1024),
        name="inverse_factor",
    )(gram)


def per_device(n, gradient, momentum, right_basis_old, token_counts):
    mats = momentum.shape[0]
    token_total = lax.psum(jnp.sum(token_counts.astype(jnp.float32)), ("fsdp", "tp"))
    width = momentum.shape[2] * lax.axis_size("tp")
    rank = right_basis_old.shape[1] * n

    basis = lax.all_gather(right_basis_old, "fsdp", axis=1, tiled=True)
    store = momentum + gradient.astype(jnp.float32) / token_total
    projected = lax.psum(jnp.einsum("mij,mkj->mik", store, basis, precision=top_precision), "tp")
    gram = lax.psum(jnp.einsum("mut,mug->mtg", projected, projected, precision=top_precision), "fsdp")
    terms = jnp.einsum("mut,muc->mtc", projected, store, precision=good_precision)
    own_rows = ring_scatter(terms, n)
    inverse = inverse_factor(gram)
    whole = lax.all_gather(own_rows, "fsdp", axis=1, tiled=True)
    orthonormal = jnp.einsum("mut,mrt->mur", projected, inverse, precision=top_precision)
    reduced = jnp.einsum("mrt,mtc->mrc", inverse, whole, precision=good_precision)
    squares = lax.psum(jnp.sum(reduced * reduced, axis=2), "tp")
    row_rms = jnp.sqrt(squares / width + epsilon)
    corrected = store - retained_fraction * jnp.einsum(
        "mur,mrc->muc", orthonormal, reduced, precision=good_precision
    )
    scaled = orthonormal * (math.sqrt(width / rank) / row_rms)[:, None, :]
    direction = jnp.einsum("mur,mrc->muc", scaled, reduced, precision=good_precision)
    rows = rank // n
    first = lax.axis_index("fsdp") * rows
    right_basis_new = (
        lax.dynamic_slice_in_dim(reduced, first, rows, 1)
        / lax.dynamic_slice_in_dim(row_rms, first, rows, 1)[:, :, None]
    )
    return (corrected, direction, right_basis_new)


def solution(mesh):
    spec = P(None, "fsdp", "tp")
    return jax.shard_map(
        functools.partial(per_device, mesh.shape["fsdp"]),
        mesh=mesh,
        in_specs=(spec, spec, spec, P(("fsdp", "tp"))),
        out_specs=(spec, spec, spec),
        check_vma=False,
    )
```

time: 1520 us -> 780 us (0.51)
  waiting for transfers between devices: 902 us -> 285 us
  Pallas kernels: 0 us -> 284 us
  other arithmetic: 258 us -> 2.36 us
  matrix products: 199 us -> 139 us
  local copies, waits for them, and re-layouts: 48.4 us -> 1.67 us
  blocking collectives: 86 us -> 46.8 us
    unnamed x6 -> x4, waiting for transfers between devices: 454 us -> 0.73 us
    pallas_call x0 -> x2, Pallas kernels: none -> 284 us  [the longest x1 210 us: ring_scatter(): pl.pallas_call(functools.partial(scatter_kernel, n, halves), out_shape=ja...]
    another operation x20 -> x0, other arithmetic: 237 us -> none  [the longest x16 154 us: per_device(): factor = jnp.linalg.cholesky(inner_products)]
    psum x2, waiting for transfers between devices: 146 us -> 19.5 us  [the longest x1 19.5 us: per_device(): lax.psum(jnp.einsum('mij,mkj->mik', store, basis, precision=top_precision...]
    dot_general x5 -> x7, matrix products: 180 us -> 139 us  [the longest x1 34 us: per_device(): jnp.einsum('mij,mkj->mik', store, basis, precision=top_precision)]
    all_gather x1 -> x0, blocking collectives: 39.2 us -> none  [per_device(): lax.all_gather(local_rms, 'fsdp', axis=0, tiled=True)]
    all_gather x2, waiting for transfers between devices: 301 us -> 265 us  [the longest x1 153 us: per_device(): basis = lax.all_gather(right_basis_old, 'fsdp', axis=1, tiled=True)]
    transpose x1 -> x0, local copies, waits for them, and re-layouts: 25.3 us -> none  [per_device(): jnp.einsum('ksf,ksu->fku', orthogonal_factor, momentum_store, precision=t...]
  transfers between devices with their start and end apart: 5 -> 4, of which waited for: 5 -> 3; matrix products, arithmetic and copies ran while one was open for 0% -> 4% of each run, Pallas kernels for 0% -> 37%
where the time goes in v1:
time: 780 us; the launch traced here: 774 us
  waiting for transfers between devices  285 us (37%)
  Pallas kernels  284 us (36%)
  matrix products  139 us (18%)
  blocking collectives  46.8 us (6%)
  between operations  14.7 us (2%)
    pallas_call x1, Pallas kernels, ring_scatter(): pl.pallas_call(functools.partial(scatter_kernel, n, halves), out_shape=ja...  210 us
    all_gather x1, waiting for transfers between devices, per_device(): basis = lax.all_gather(right_basis_old, 'fsdp', axis=1, tiled=True)  153 us
    all_gather x1, waiting for transfers between devices, per_device(): whole = lax.all_gather(own_rows, 'fsdp', axis=1, tiled=True)  112 us
    pallas_call x1, Pallas kernels, inverse_factor(): pl.pallas_call(factor_kernel, out_shape=jax.ShapeDtypeStruct(gram.shape,...  74 us
    psum x1, blocking collectives, per_device(): lax.psum(jnp.sum(token_counts.astype(jnp.float32)), ('fsdp', 'tp'))  44.4 us
    dot_general x1, matrix products, per_device(): jnp.einsum('mij,mkj->mik', store, basis, precision=top_precision)  34 us
    dot_general x1, matrix products, per_device(): jnp.einsum('mur,mrc->muc', orthonormal, reduced, precision=good_precision)  27.9 us
    dot_general x1, matrix products, per_device(): jnp.einsum('mut,muc->mtc', projected, store, precision=good_precision)  23.3 us
  transfers between devices with their start and end apart: 4, of which 3 were waited for; matrix products, arithmetic and copies ran while one was open for 4% of the time, Pallas kernels for 37%

profile of v1, /device:TPU:0, one launch (start us, length us, event | category | flops | bytes accessed | tf_op | source)
XLA Modules:
  0.0 774.3 jit_solution(5960028328625453386)
XLA Ops:
  7.2 0.0 all-gather.3.cloned.1.call-start
  7.2 0.7 all-gather.3.cloned.1.call-update
  7.9 0.0 all-reduce.3.cloned.1.call-start
  8.6 44.4 %psum.28 = f32[]{:T(128)} all-reduce(f32[]{:T(128)} %bitcast), channel_id=1, replica_groups=mesh['fsdp'=16,'tp'=2] {'fsdp','tp'}, use_global_device_ids=true, to_apply=%region_0.0 | all-reduce | flops 1 | bytes 8 | tf_op jit(solution)/shard_map/psum | solution.py:201
  53.0 153.3 %all-gather.3.cloned.1.call-done = f32[2,512,4096]{2,1,0:T(8,128)} async-done(((f32[2,32,4096]{2,1,0:T(8,128)}), f32[2,512,4096]{2,1,0:T(8,128)}) %all-gather.3.cloned.1.call-update) | async-done | bytes 16777232 | tf_op jit(solution)/shard_map/all_gather | solution.py:205
  206.2 34.0 %fusion.4 = f32[2,512,512]{2,1,0:T(8,128)} fusion(f32[2,512,4096]{2,1,0:T(8,128)} %all-gather.3.cloned.1.call-done, f32[2,512,4096]{2,1,0:T(8,128)} %param.5, bf16[2,512,4096]{2,1,0:T(8,128)(2,1)} %param.4, f32[]{:T(128)} %psum.28), kind=kOutput, calls=%fused_computation.11 | convolution fusion | flops 25782386688 | bytes 44040196 | tf_op jit(solution)/shard_map/mij,mkj->mik/dot_general | solution.py:207
  240.2 0.0 all-reduce.3.cloned.1.call-update
  240.3 0.0 all-reduce.5.cloned.1.call-start
  240.3 19.5 %all-reduce.3.cloned.1.call-done = f32[2,512,512]{2,1,0:T(8,128)} async-done(((f32[2,512,512]{2,1,0:T(8,128)}), f32[2,512,512]{2,1,0:T(8,128)}) %all-reduce.3.cloned.1.call-update) | async-done | bytes 2097168 | tf_op jit(solution)/shard_map/psum | solution.py:207
  259.8 7.1 fusion.5
  266.9 0.0 all-reduce.5.cloned.1.call-update
  266.9 0.3 all-gather.5.cloned.1.call-start
  267.2 23.3 %fusion.3.terms = f32[2,512,4096]{2,1,0:T(8,128)} fusion(f32[2,512,512]{2,1,0:T(8,128)} %all-reduce.3.cloned.1.call-done, f32[2,512,4096]{2,1,0:T(8,128)} %param.5, bf16[2,512,4096]{2,1,0:T(8,128)(2,1)} %param.4, f32[]{:T(128)} %psum.28), kind=kOutput, calls=%fused_computation.10 | convolution fusion | flops 12897484800 | bytes 44040196 | tf_op jit(solution)/shard_map/mut,muc->mtc/dot_general | solution.py:209
  290.5 210.2 %ring_scatter.1 = f32[2,32,4096]{2,1,0:T(8,128)} custom-call(f32[2,512,4096]{2,1,0:T(8,128)} %fusion.3.terms), custom_call_target="tpu_custom_call" | custom-call | flops 4194304 | bytes 167772160 | tf_op jit(solution)/shard_map/ring_scatter/pallas_call | solution.py:104
  500.7 0.0 all-gather.5.cloned.1.call-update
  500.7 0.0 all-reduce.5.cloned.1.call-done.gram
  500.8 0.0 copy-start
  500.8 1.6 copy-done
  502.3 0.0 copy-start.1
  502.3 74.0 %inverse_factor.1 = f32[2,512,512]{2,1,0:T(8,128)S(1)} custom-call(f32[2,512,512]{2,1,0:T(8,128)S(1)} %copy-done), custom_call_target="tpu_custom_call" | custom-call | flops 80000000000 | bytes 4194304 | tf_op jit(solution)/shard_map/inverse_factor/pallas_call | solution.py:187
  576.4 0.0 copy-done.1
  576.4 4.9 fusion.6
  581.2 111.8 %all-gather.5.cloned.1.call-done = f32[2,512,4096]{2,1,0:T(8,128)} async-done(((f32[2,32,4096]{2,1,0:T(8,128)}), f32[2,512,4096]{2,1,0:T(8,128)}) %all-gather.5.cloned.1.call-update) | async-done | bytes 16777232 | tf_op jit(solution)/shard_map/all_gather | solution.py:212
  693.0 20.7 %multiply_reduce_fusion = (f32[2,512]{1,0:T(2,128)S(1)}, f32[2,512,4096]{2,1,0:T(8,128)}) fusion(f32[2,512,512]{2,1,0:T(8,128)S(1)} %inverse_factor.1, f32[2,512,4096]{2,1,0:T(8,128)} %all-gather.5.cloned.1.call-done), kind=kOutput, calls=%fused_computation | convolution fusion | flops 12893289472 | bytes 35655680 | tf_op jit(solution)/shard_map/mrt,mtc->mrc/dot_general | solution.py:214
  713.7 2.4 psum.31
  716.2 0.0 copy-start.2
  716.2 27.9 %multiply_subtract_fusion = f32[2,512,4096]{2,1,0:T(8,128)} fusion(f32[2,512,512]{2,1,0:T(8,128)} %fusion.6, f32[2,512,4096]{2,1,0:T(8,128)} %get-tuple-element.6, f32[2,512,4096]{2,1,0:T(8,128)} %param.5, f32[]{:T(128)} %psum.28, bf16[2,512,4096]{2,1,0:T(8,128)(2,1)} %param.4), kind=kOutput, calls=%fused_computation.1 | convolution fusion | flops 12905873408 | bytes 60817412 | tf_op jit(solution)/shard_map/mur,mrc->muc/dot_general | solution.py:217
  744.1 0.0 copy-done.2
  744.1 21.0 %fusion = f32[2,512,4096]{2,1,0:T(8,128)} fusion(f32[2,512,4096]{2,1,0:T(8,128)} %get-tuple-element.6, f32[2,512,512]{2,1,0:T(8,128)S(1)} %copy-done.2, f32[2,512]{1,0:T(2,128)S(1)} %get-tuple-element.4), kind=kOutput, calls=%fused_computation.3 | convolution fusion | flops 12885426176 | bytes 35655680 | tf_op jit(solution)/shard_map/mur,mrc->muc/dot_general | solution.py:221
  765.1 0.1 constant_dynamic-slice_fusion
  765.1 2.3 dynamic-slice_divide_fusion
  (1 shorter events, 0.0 us)
Async XLA Ops:
  7.2 199.1 %all-gather.3.cloned.1.call-start = ((), (), s32[]{:S(2)}) async-start(), calls=%async_computation | async-start | bytes 17825792 | tf_op jit(solution)/shard_map/all_gather | solution.py:205
  7.9 251.9 %all-reduce.3.cloned.1.call-start = ((), (), s32[]{:S(2)}) async-start(), calls=%async_computation.1 | async-start | bytes 4194304 | tf_op jit(solution)/shard_map/psum | solution.py:207
  240.3 260.5 %all-reduce.5.cloned.1.call-start = ((), (), s32[]{:S(2)}) async-start(), calls=%async_computation.2 | async-start | bytes 4194304 | tf_op jit(solution)/shard_map/psum | solution.py:208
  266.9 426.1 %all-gather.5.cloned.1.call-start = ((), (), s32[]{:S(2)}) async-start(), calls=%async_computation.3 | async-start | bytes 17825792 | tf_op jit(solution)/shard_map/all_gather | solution.py:212
  500.8 1.6 copy-start
  502.3 74.0 %copy-start.1 = (f32[2,512,512]{2,1,0:T(8,128)S(1)}, f32[2,512,512]{2,1,0:T(8,128)}, u32[]{:S(2)}) copy-start(f32[2,512,512]{2,1,0:T(8,128)} %all-reduce.3.cloned.1.call-done) | copy-start | bytes 6291460
  716.2 27.9 %copy-start.2 = (f32[2,512,512]{2,1,0:T(8,128)S(1)}, f32[2,512,512]{2,1,0:T(8,128)}, u32[]{:S(2)}) copy-start(f32[2,512,512]{2,1,0:T(8,128)} %fusion.6) | copy-start | bytes 6291460
Sparse Core Ops, SparseCore 0:
  10.8 195.4 all-gather.2
  240.4 19.3 all-reduce.2
  267.0 146.4 all-reduce.4
  500.8 192.1 all-gather.4

commit v2 on v1

--- a/solution.py
+++ b/solution.py
@@ -100,7 +100,7 @@
 
 def ring_scatter(terms, n):
     mats, rank, width = terms.shape
-    rows, halves = rank // n, 2
+    rows, halves = rank // n, 4
     return pl.pallas_call(
         functools.partial(scatter_kernel, n, halves),
         out_shape=jax.ShapeDtypeStruct((mats, rows, width), jnp.float32),
@@ -204,7 +204,7 @@
 
     basis = lax.all_gather(right_basis_old, "fsdp", axis=1, tiled=True)
     store = momentum + gradient.astype(jnp.float32) / token_total
-    projected = lax.psum(jnp.einsum("mij,mkj->mik", store, basis, precision=top_precision), "tp")
+    projected = lax.psum(jnp.einsum("mij,mkj->mik", store, basis, precision=good_precision), "tp")
     gram = lax.psum(jnp.einsum("mut,mug->mtg", projected, projected, precision=top_precision), "fsdp")
     terms = jnp.einsum("mut,muc->mtc", projected, store, precision=good_precision)
     own_rows = ring_scatter(terms, n)

time: 780 us -> 768 us (0.985)
  matrix products: 139 us -> 125 us
    dot_general x1, matrix products: 34 us -> 20.7 us  [per_device(): jnp.einsum('mij,mkj->mik', store, basis, precision=good_precision)]
where the time goes in v2:
time: 768 us; the launch traced here: 762 us
  waiting for transfers between devices  285 us (37%)
  Pallas kernels  285 us (37%)
  matrix products  125 us (16%)
  blocking collectives  46.8 us (6%)
  between operations  14.7 us (2%)
    pallas_call x1, Pallas kernels, ring_scatter(): pl.pallas_call(functools.partial(scatter_kernel, n, halves), out_shape=ja...  211 us
    all_gather x1, waiting for transfers between devices, per_device(): basis = lax.all_gather(right_basis_old, 'fsdp', axis=1, tiled=True)  153 us
    all_gather x1, waiting for transfers between devices, per_device(): whole = lax.all_gather(own_rows, 'fsdp', axis=1, tiled=True)  112 us
    pallas_call x1, Pallas kernels, inverse_factor(): pl.pallas_call(factor_kernel, out_shape=jax.ShapeDtypeStruct(gram.shape,...  74 us
    psum x1, blocking collectives, per_device(): lax.psum(jnp.sum(token_counts.astype(jnp.float32)), ('fsdp', 'tp'))  44.4 us
    dot_general x1, matrix products, per_device(): jnp.einsum('mur,mrc->muc', orthonormal, reduced, precision=good_precision)  27.9 us
    dot_general x1, matrix products, per_device(): jnp.einsum('mut,muc->mtc', projected, store, precision=good_precision)  23.3 us
    dot_general x1, matrix products, per_device(): jnp.einsum('mur,mrc->muc', scaled, reduced, precision=good_precision)  21 us
  transfers between devices with their start and end apart: 4, of which 3 were waited for; matrix products, arithmetic and copies ran while one was open for 4% of the time, Pallas kernels for 37%

profile of v2, /device:TPU:0, one launch (start us, length us, event | category | flops | bytes accessed | tf_op | source)
XLA Modules:
  0.0 761.8 jit_solution(8329155641292580580)
XLA Ops:
  7.2 0.0 all-gather.3.cloned.1.call-start
  7.2 0.7 all-gather.3.cloned.1.call-update
  7.9 0.0 all-reduce.3.cloned.1.call-start
  8.6 44.4 %psum.28 = f32[]{:T(128)} all-reduce(f32[]{:T(128)} %bitcast), channel_id=1, replica_groups=mesh['fsdp'=16,'tp'=2] {'fsdp','tp'}, use_global_device_ids=true, to_apply=%region_0.0 | all-reduce | flops 1 | bytes 8 | tf_op jit(solution)/shard_map/psum | solution.py:201
  53.0 153.3 %all-gather.3.cloned.1.call-done = f32[2,512,4096]{2,1,0:T(8,128)} async-done(((f32[2,32,4096]{2,1,0:T(8,128)}), f32[2,512,4096]{2,1,0:T(8,128)}) %all-gather.3.cloned.1.call-update) | async-done | bytes 16777232 | tf_op jit(solution)/shard_map/all_gather | solution.py:205
  206.2 20.7 %fusion.4 = f32[2,512,512]{2,1,0:T(8,128)} fusion(f32[2,512,4096]{2,1,0:T(8,128)} %all-gather.3.cloned.1.call-done, f32[2,512,4096]{2,1,0:T(8,128)} %param.5, bf16[2,512,4096]{2,1,0:T(8,128)(2,1)} %param.4, f32[]{:T(128)} %psum.28), kind=kOutput, calls=%fused_computation.11 | convolution fusion | flops 12897484800 | bytes 44040196 | tf_op jit(solution)/shard_map/mij,mkj->mik/dot_general | solution.py:207
  226.9 0.0 all-reduce.3.cloned.1.call-update
  226.9 0.0 all-reduce.5.cloned.1.call-start
  227.0 19.5 %all-reduce.3.cloned.1.call-done = f32[2,512,512]{2,1,0:T(8,128)} async-done(((f32[2,512,512]{2,1,0:T(8,128)}), f32[2,512,512]{2,1,0:T(8,128)}) %all-reduce.3.cloned.1.call-update) | async-done | bytes 2097168 | tf_op jit(solution)/shard_map/psum | solution.py:207
  246.5 7.1 fusion.5
  253.5 0.0 all-reduce.5.cloned.1.call-update
  253.6 0.3 all-gather.5.cloned.1.call-start
  253.9 23.3 %fusion.3.terms = f32[2,512,4096]{2,1,0:T(8,128)} fusion(f32[2,512,512]{2,1,0:T(8,128)} %all-reduce.3.cloned.1.call-done, f32[2,512,4096]{2,1,0:T(8,128)} %param.5, bf16[2,512,4096]{2,1,0:T(8,128)(2,1)} %param.4, f32[]{:T(128)} %psum.28), kind=kOutput, calls=%fused_computation.10 | convolution fusion | flops 12897484800 | bytes 44040196 | tf_op jit(solution)/shard_map/mut,muc->mtc/dot_general | solution.py:209
  277.2 211.3 %ring_scatter.1 = f32[2,32,4096]{2,1,0:T(8,128)} custom-call(f32[2,512,4096]{2,1,0:T(8,128)} %fusion.3.terms), custom_call_target="tpu_custom_call" | custom-call | flops 4194304 | bytes 167772160 | tf_op jit(solution)/shard_map/ring_scatter/pallas_call | solution.py:104
  488.5 0.0 all-gather.5.cloned.1.call-update
  488.5 0.0 all-reduce.5.cloned.1.call-done.gram
  488.5 0.0 copy-start
  488.5 1.6 copy-done
  490.1 0.0 copy-start.1
  490.1 74.0 %inverse_factor.1 = f32[2,512,512]{2,1,0:T(8,128)S(1)} custom-call(f32[2,512,512]{2,1,0:T(8,128)S(1)} %copy-done), custom_call_target="tpu_custom_call" | custom-call | flops 80000000000 | bytes 4194304 | tf_op jit(solution)/shard_map/inverse_factor/pallas_call | solution.py:187
  564.2 0.0 copy-done.1
  564.2 4.9 fusion.6
  569.0 111.5 %all-gather.5.cloned.1.call-done = f32[2,512,4096]{2,1,0:T(8,128)} async-done(((f32[2,32,4096]{2,1,0:T(8,128)}), f32[2,512,4096]{2,1,0:T(8,128)}) %all-gather.5.cloned.1.call-update) | async-done | bytes 16777232 | tf_op jit(solution)/shard_map/all_gather | solution.py:212
  680.5 20.7 %multiply_reduce_fusion = (f32[2,512]{1,0:T(2,128)S(1)}, f32[2,512,4096]{2,1,0:T(8,128)}) fusion(f32[2,512,512]{2,1,0:T(8,128)S(1)} %inverse_factor.1, f32[2,512,4096]{2,1,0:T(8,128)} %all-gather.5.cloned.1.call-done), kind=kOutput, calls=%fused_computation | convolution fusion | flops 12893289472 | bytes 35655680 | tf_op jit(solution)/shard_map/mrt,mtc->mrc/dot_general | solution.py:214
  701.2 2.4 psum.31
  703.7 0.0 copy-start.2
  703.7 27.9 %multiply_subtract_fusion = f32[2,512,4096]{2,1,0:T(8,128)} fusion(f32[2,512,512]{2,1,0:T(8,128)} %fusion.6, f32[2,512,4096]{2,1,0:T(8,128)} %get-tuple-element.6, f32[2,512,4096]{2,1,0:T(8,128)} %param.5, f32[]{:T(128)} %psum.28, bf16[2,512,4096]{2,1,0:T(8,128)(2,1)} %param.4), kind=kOutput, calls=%fused_computation.1 | convolution fusion | flops 12905873408 | bytes 60817412 | tf_op jit(solution)/shard_map/mur,mrc->muc/dot_general | solution.py:217
  731.6 0.0 copy-done.2
  731.6 21.0 %fusion = f32[2,512,4096]{2,1,0:T(8,128)} fusion(f32[2,512,4096]{2,1,0:T(8,128)} %get-tuple-element.6, f32[2,512,512]{2,1,0:T(8,128)S(1)} %copy-done.2, f32[2,512]{1,0:T(2,128)S(1)} %get-tuple-element.4), kind=kOutput, calls=%fused_computation.3 | convolution fusion | flops 12885426176 | bytes 35655680 | tf_op jit(solution)/shard_map/mur,mrc->muc/dot_general | solution.py:221
  752.6 0.1 constant_dynamic-slice_fusion
  752.7 2.3 dynamic-slice_divide_fusion
  (1 shorter events, 0.0 us)
Async XLA Ops:
  7.2 199.1 %all-gather.3.cloned.1.call-start = ((), (), s32[]{:S(2)}) async-start(), calls=%async_computation | async-start | bytes 17825792 | tf_op jit(solution)/shard_map/all_gather | solution.py:205
  7.9 238.6 %all-reduce.3.cloned.1.call-start = ((), (), s32[]{:S(2)}) async-start(), calls=%async_computation.1 | async-start | bytes 4194304 | tf_op jit(solution)/shard_map/psum | solution.py:207
  226.9 261.6 %all-reduce.5.cloned.1.call-start = ((), (), s32[]{:S(2)}) async-start(), calls=%async_computation.2 | async-start | bytes 4194304 | tf_op jit(solution)/shard_map/psum | solution.py:208
  253.6 427.0 %all-gather.5.cloned.1.call-start = ((), (), s32[]{:S(2)}) async-start(), calls=%async_computation.3 | async-start | bytes 17825792 | tf_op jit(solution)/shard_map/all_gather | solution.py:212
  488.5 1.6 copy-start
  490.1 74.0 %copy-start.1 = (f32[2,512,512]{2,1,0:T(8,128)S(1)}, f32[2,512,512]{2,1,0:T(8,128)}, u32[]{:S(2)}) copy-start(f32[2,512,512]{2,1,0:T(8,128)} %all-reduce.3.cloned.1.call-done) | copy-start | bytes 6291460
  703.7 27.9 %copy-start.2 = (f32[2,512,512]{2,1,0:T(8,128)S(1)}, f32[2,512,512]{2,1,0:T(8,128)}, u32[]{:S(2)}) copy-start(f32[2,512,512]{2,1,0:T(8,128)} %fusion.6) | copy-start | bytes 6291460
Sparse Core Ops, SparseCore 0:
  10.8 195.4 all-gather.2
  227.0 19.3 all-reduce.2
  253.7 146.6 all-reduce.4
  488.6 191.8 all-gather.4
